TPU v7x, 32 devices: a whole 2x2x4 slice. The times are simulated.
32 devices in a mesh: groups: 2 (over x), chan: 16 (over z, y, core).
Axes of the slice: x: 2, y: 2, z: 4, core: 2. Of those that a mesh axis runs over, the one named last changes fastest.
Arguments:
- voltages: int32 [4096, 79, 2048], P(('groups', 'chan')), parts along dimension 0, may hold values from -96 to 96, as said below
- input_mask: int32 [4096], P(('groups', 'chan')), parts along dimension 0, may hold values 0 or 1
- fir_taps: float32 [16, 2048], replicated, may hold values from -1.5 to 1.5
Outputs:
- visibilities: bfloat16 [32768, 2048], P(('groups', 'chan')), parts along dimension 0
There are 2 independent parts, one for each index of `groups`. A program takes and returns all parts, laid end to end along the dimension named above; an argument that names none is the same for every part. Nothing has to cross between parts.
Inputs may be any that keep to these rules, and one draw needn't show every extreme that they name: `voltages`: 8-bit voltage samples; each input's amplitude, colour and share of a common signal differ.
All inputs are finite; a program needn't handle non-finite values. No bound on the sum of `input_mask` on one device may be relied on, other than what follows from the above.
Results may differ from a plain program's by a relative error of at most 0.006.
Values may be sent and summed in bfloat16 or wider, within the bound.
A program may use at most 320 MiB of HBM per device.

v0:
```python
from functools import reduce
import math
import jax
import jax.numpy as jnp
from jax import lax
from jax.sharding import PartitionSpec as P

INPUTS = 2048
NFFT = 2048
TAPS = 16
SPEC = 64
epsilon = 1e-05


def swapped(value, axis, stride):
    return lax.ppermute(value, axis, [(i, i ^ 1 << stride) for i in range(lax.axis_size(axis))])


def dft_matrix(length, channels):
    column = jnp.arange(length, dtype=jnp.int32)[:, None]
    channel = jnp.arange(1, channels + 1, dtype=jnp.int32)[None, :]
    phases = column * channel % length
    angles = phases.astype(jnp.float32) * (2.0 * math.pi / length)
    return jnp.concatenate([jnp.cos(angles), -jnp.sin(angles)], axis=1).astype(jnp.bfloat16)


def add_terms(left, right):
    return left + right


def polyphase(voltages, input_mask, fir_taps):
    samples = (voltages * input_mask[:, None, None]).astype(jnp.bfloat16)
    terms = [
        fir_taps[offset][None, None, :] * samples[:, offset : offset + SPEC, :]
        for offset in range(TAPS)
    ]
    filtered = reduce(add_terms, terms)
    return filtered.astype(jnp.bfloat16)


def contract(left, right):
    return lax.dot_general(
        left, right, (((1,), (1,)), ((), ())), preferred_element_type=jnp.float32
    )


def on_device(voltages, input_mask, fir_taps):
    devices = lax.axis_size("chan")
    channels = devices // 2
    local_inputs = voltages.shape[0]
    filtered = polyphase(voltages, input_mask, fir_taps)
    spectra = jnp.einsum(
        "isn,nk->iks", filtered, dft_matrix(NFFT, channels), preferred_element_type=jnp.float32
    )
    squares = jnp.sum(spectra * spectra, axis=(0, 2))
    band_partial = squares[:channels] + squares[channels:]
    band_total = lax.psum(band_partial, "chan")
    channel_gain = lax.rsqrt(band_total / (INPUTS * SPEC) + epsilon)
    equalized = (spectra * jnp.concatenate([channel_gain, channel_gain])[None, :, None]).astype(
        jnp.bfloat16
    )
    by_channel = equalized.reshape(local_inputs, 2, channels, SPEC)
    parity = lax.axis_index("chan") % 2
    half_rows = INPUTS // 2
    half_spec = SPEC // 2
    outgoing = by_channel.reshape(local_inputs, 2, channels, 2, half_spec)
    outgoing = outgoing.transpose(2, 3, 0, 1, 4).reshape(devices, local_inputs, SPEC)
    received = lax.all_to_all(outgoing, "chan", split_axis=0, concat_axis=1, tiled=True)[0]
    real_part = received[:, :half_spec]
    imag_part = received[:, half_spec:]
    rotated = jnp.concatenate([imag_part, -real_part], axis=1)
    real_vis = contract(received, received)
    imag_vis = contract(rotated, received)
    row_index = jnp.arange(INPUTS, dtype=jnp.int32)[:, None]
    column_index = jnp.arange(INPUTS, dtype=jnp.int32)[None, :]
    packed = jnp.where(column_index <= row_index, real_vis, imag_vis)
    partner_rows = lax.dynamic_slice_in_dim(packed, (1 - parity) * half_rows, half_rows, 0)
    own_rows = lax.dynamic_slice_in_dim(packed, parity * half_rows, half_rows, 0)
    summed = own_rows + swapped(partner_rows, "chan", 0)
    return (summed / SPEC).astype(jnp.bfloat16)


def solution(mesh):
    return jax.shard_map(
        on_device,
        mesh=mesh,
        in_specs=(P(("groups", "chan"), None, None), P(("groups", "chan")), P()),
        out_specs=P(("groups", "chan"), None),
        check_vma=False,
    )
```

profile of v0, /device:TPU:0, one launch (start us, length us, event | category | flops | bytes accessed | tf_op | source)
XLA Modules:
  0.0 349.4 jit_solution(1774210906190760884)
XLA Ops:
  0.0 1.9 fusion.17
  1.9 1.0 cosine_convert_fusion
  2.8 40.1 %multiply_convert_fusion = bf16[128,79,2048]{2,0,1:T(8,128)(2,1)} fusion(s32[128,79,2048]{2,0,1:T(8,128)} %param.3, s32[128]{0:T(128)} %param.4), kind=kLoop, calls=%fused_computation | loop fusion | flops 41418752 | bytes 124256768 | tf_op jit(solution)/shard_map/convert_element_type | solution.py:32
  42.9 0.0 copy-start
  43.0 0.0 copy-start.1
  43.0 200.1 %add_convert_fusion.1.clone.5 = bf16[128,64,2048]{2,0,1:T(8,128)(2,1)} fusion(bf16[128,79,2048]{2,0,1:T(8,128)(2,1)} %multiply_convert_fusion, f32[2048]{0:T(1024)S(1)} %bitcast.59, f32[2048]{0:T(1024)S(1)} %bitcast.60, f32[2048]{0:T(1024)S(1)} %bitcast.46, f32[2048]{0:T(1024)S(1)} %bitcast.47, f32[2048]{0:T(1024)S(1)} %bitcast.48, ...), kind=kLoop, calls=%fused_computation.1.clone.clone.clone.clone.2 | loop fusion | flops 805306368 | bytes 570556416 | tf_op jit(solution)/shard_map/reduce_sum | solution.py:55
  243.1 0.0 copy-done
  243.1 0.0 copy-done.1
  243.1 14.6 %multiply_reduce_fusion = (f32[16]{0:T(128)S(1)}, f32[16,128,64]{1,0,2:T(8,128)S(1)}) fusion(bf16[2048,8]{0,1:T(8,128)(2,1)S(1)} %copy-done.1, bf16[2048,8]{0,1:T(8,128)(2,1)S(1)} %copy-done, bf16[128,64,2048]{2,0,1:T(8,128)(2,1)} %add_convert_fusion.1.clone.5), kind=kOutput, calls=%fused_computation.7 | convolution fusion | flops 537264128 | bytes 34144320 | tf_op jit(solution)/shard_map/isn,nk->iks/dot_general | solution.py:52
  257.7 0.1 slice_add_fusion
  257.8 34.9 %psum.7 = f32[8]{0:T(128)S(1)} all-reduce(f32[8]{0:T(128)S(1)} %slice_add_fusion), channel_id=1, replica_groups=mesh['groups'=2,'chan'=16] {'chan'}, use_global_device_ids=true, to_apply=%region_1.2 | all-reduce | flops 8 | bytes 64 | tf_op jit(solution)/shard_map/psum | solution.py:57
  292.7 0.1 pad_maximum_fusion
  292.8 0.1 multiply_convert_fusion.2
  292.9 0.8 copy.5
  293.7 3.7 %all-to-all-start = ((bf16[16,128,64]{1,2,0:T(8,128)(2,1)}), bf16[16,128,64]{1,2,0:T(8,128)(2,1)S(1)}, u32[]{:S(2)}, u32[]{:S(2)}) async-start(bf16[16,128,64]{1,2,0:T(8,128)(2,1)} %bitcast.20), calls=%async_computation | async-start | bytes 524288 | tf_op jit(solution)/shard_map/all_to_all | solution.py:68
  297.4 9.8 %all-to-all-done = bf16[16,128,64]{1,2,0:T(8,128)(2,1)S(1)} async-done(((bf16[16,128,64]{1,2,0:T(8,128)(2,1)}), bf16[16,128,64]{1,2,0:T(8,128)(2,1)S(1)}, u32[]{:S(2)}, u32[]{:S(2)}) %all-to-all-start) | async-done | bytes 262176 | tf_op jit(solution)/shard_map/all_to_all | solution.py:68
  307.3 2.4 fusion.15
  309.7 8.6 %fusion.1 = f32[2048,2048]{1,0:T(8,128)} fusion(f32[2048,2048]{1,0:T(8,128)S(1)} %fusion.15, bf16[2048,32]{0,1:T(8,128)(2,1)S(1)} %get-tuple-element.6, bf16[2048,32]{0,1:T(8,128)(2,1)S(1)} %get-tuple-element.5, bf16[16,128,64]{1,2,0:T(8,128)(2,1)S(1)} %all-to-all-done), kind=kOutput, calls=%fused_computation.4 | convolution fusion | flops 545783808 | bytes 34078720 | tf_op jit(solution)/shard_map/dot_general | solution.py:42
  318.3 7.7 %constant_dynamic-slice_fusion = f32[1024,2048]{1,0:T(8,128)} fusion(f32[2048,2048]{1,0:T(8,128)} %fusion.1, s32[]{:T(128)S(6)} %select_n.29), kind=kLoop, calls=%fused_computation.30 | loop fusion | bytes 16777220 | tf_op jit(solution)/shard_map/dynamic_slice | solution.py:77
  326.0 0.0 collective-permute-start
  326.0 13.5 %collective-permute-done = f32[1024,2048]{1,0:T(8,128)} collective-permute-done((f32[1024,2048]{1,0:T(8,128)}, f32[1024,2048]{1,0:T(8,128)}, u32[]{:S(2)}, u32[]{:S(2)}) %collective-permute-start) | collective-permute-done | bytes 8388640 | tf_op jit(solution)/shard_map/ppermute | solution.py:16
  339.5 10.0 %multiply_convert_fusion.1 = bf16[1024,2048]{1,0:T(8,128)(2,1)} fusion(f32[1024,2048]{1,0:T(8,128)} %collective-permute-done, f32[2048,2048]{1,0:T(8,128)} %fusion.1, s32[]{:T(128)S(6)} %select_n.28), kind=kLoop, calls=%fused_computation.5 | loop fusion | flops 6291456 | bytes 20971524 | tf_op jit(solution)/shard_map/convert_element_type | solution.py:80
  (4 shorter events, 0.1 us)
Async XLA Ops:
  42.9 200.1 %copy-start = (bf16[2048,8]{0,1:T(8,128)(2,1)S(1)}, bf16[2048,8]{0,1:T(8,128)(2,1)}, u32[]{:S(2)}) copy-start(bf16[2048,8]{0,1:T(8,128)(2,1)} %get-tuple-element.23) | copy-start | bytes 98308
  43.0 200.1 %copy-start.1 = (bf16[2048,8]{0,1:T(8,128)(2,1)S(1)}, bf16[2048,8]{0,1:T(8,128)(2,1)}, u32[]{:S(2)}) copy-start(bf16[2048,8]{0,1:T(8,128)(2,1)} %get-tuple-element.24) | copy-start | bytes 98308
  293.7 13.5 %all-to-all-start = ((bf16[16,128,64]{1,2,0:T(8,128)(2,1)}), bf16[16,128,64]{1,2,0:T(8,128)(2,1)S(1)}, u32[]{:S(2)}, u32[]{:S(2)}) async-start(bf16[16,128,64]{1,2,0:T(8,128)(2,1)} %bitcast.20), calls=%async_computation | async-start | bytes 524288 | tf_op jit(solution)/shard_map/all_to_all | solution.py:68
  326.0 13.5 %collective-permute-start = (f32[1024,2048]{1,0:T(8,128)}, f32[1024,2048]{1,0:T(8,128)}, u32[]{:S(2)}, u32[]{:S(2)}) collective-permute-start(f32[1024,2048]{1,0:T(8,128)} %constant_dynamic-slice_fusion), channel_id=1, source_target_pairs={{0,1},{1,0},{2,3},{3,2},{4,5},{5,4},{6,7},{7,6},{8,9},{9,8},{10,11... | collective-permute-start | bytes 25165832 | tf_op jit(solution)/shard_map/ppermute | solution.py:16
where the time goes:
time: 350 us; the launch traced here: 349 us
  other arithmetic  251 us (72%)
  blocking collectives  34.9 us (10%)
  matrix products  25.6 us (7%)
  waiting for transfers between devices  23.3 us (7%)
  local copies, waits for them, and re-layouts  10.4 us (3%)
  starting transfers between devices  3.72 us (1%)
    reduce_sum x1, other arithmetic, on_device(): squares = jnp.sum(spectra * spectra, axis=(0, 2))  200 us
    convert_element_type x1, other arithmetic, polyphase(): samples = (voltages * input_mask[:, None, None]).astype(jnp.bfloat16)  40.1 us
    psum x1, blocking collectives, on_device(): band_total = lax.psum(band_partial, 'chan')  34.9 us
    dot_general x1, matrix products, on_device(): jnp.einsum('isn,nk->iks', filtered, dft_matrix(NFFT, channels), preferred...  14.6 us
    ppermute x1, waiting for transfers between devices, swapped(): lax.ppermute(value, axis, [(i, i ^ 1 << stride) for i in range(lax.axis_s...  13.5 us
    dot_general x2, matrix products, contract(): lax.dot_general(left, right, (((1,), (1,)), ((), ())), preferred_element_...  10.9 us
    convert_element_type x1, other arithmetic, on_device(): return (summed / SPEC).astype(jnp.bfloat16)  9.98 us
    all_to_all x1, waiting for transfers between devices, on_device(): lax.all_to_all(outgoing, 'chan', split_axis=0, concat_axis=1, tiled=True)[0]  9.81 us
  transfers between devices with their start and end apart: 2, of which 2 were waited for; matrix products, arithmetic and copies ran while one was open for 0% of the time, Pallas kernels for 0%

commit v1 on v0

--- a/solution.py
+++ b/solution.py
@@ -10,6 +10,29 @@
 TAPS = 16
 SPEC = 64
 epsilon = 1e-05
+
+
+def in_blocks(array, dim, devices):
+    lengths = array.shape
+    blocks = array.reshape(*lengths[:dim], devices, lengths[dim] // devices, *lengths[dim + 1 :])
+    return jnp.moveaxis(blocks, dim, 0)
+
+
+def joined_along(blocks, dim):
+    dims = list(blocks.shape[1:])
+    dims[dim] *= blocks.shape[0]
+    return jnp.moveaxis(blocks, 0, dim).reshape(dims)
+
+
+def rotated_exchange(array, axis, split_dim, concat_dim):
+    size, place = (lax.axis_size(axis), lax.axis_index(axis))
+    pieces = in_blocks(array, split_dim, size)
+    finished = [pieces[place]]
+    for step in range(1, size):
+        sent = pieces[(place + step) % size]
+        finished.append(lax.ppermute(sent, axis, [(i, (i + step) % size) for i in range(size)]))
+    pieces = jnp.stack(finished)[(place - jnp.arange(size)) % size]
+    return joined_along(pieces, concat_dim)
 
 
 def swapped(value, axis, stride):
@@ -65,7 +88,7 @@
     half_spec = SPEC // 2
     outgoing = by_channel.reshape(local_inputs, 2, channels, 2, half_spec)
     outgoing = outgoing.transpose(2, 3, 0, 1, 4).reshape(devices, local_inputs, SPEC)
-    received = lax.all_to_all(outgoing, "chan", split_axis=0, concat_axis=1, tiled=True)[0]
+    received = rotated_exchange(outgoing, "chan", 0, 1)[0]
     real_part = received[:, :half_spec]
     imag_part = received[:, half_spec:]
     rotated = jnp.concatenate([imag_part, -real_part], axis=1)

time: 350 us -> 359 us (1.026)
  starting transfers between devices: 3.72 us -> 16.5 us
  waiting for transfers between devices: 23.3 us -> 19.5 us
    ppermute x0 -> x15, starting transfers between devices: none -> 14.9 us  [rotated_exchange(): lax.ppermute(sent, axis, [(i, (i + step) % size) for i in range(size)])]
    all_to_all x1 -> x0, waiting for transfers between devices: 9.81 us -> none  [on_device(): lax.all_to_all(outgoing, 'chan', split_axis=0, concat_axis=1, tiled=True)[0]]
    ppermute x0 -> x15, waiting for transfers between devices: none -> 6.34 us  [rotated_exchange(): lax.ppermute(sent, axis, [(i, (i + step) % size) for i in range(size)])]
    all_to_all x1 -> x0, starting transfers between devices: 3.71 us -> none  [on_device(): lax.all_to_all(outgoing, 'chan', split_axis=0, concat_axis=1, tiled=True)[0]]
  transfers between devices with their start and end apart: 2 -> 16, of which waited for: 2 -> 3; matrix products, arithmetic and copies ran while one was open for 0% -> 0% of each run, Pallas kernels for 0% -> 0%
where the time goes in v1:
time: 359 us
  other arithmetic  252 us (70%)
  blocking collectives  34.9 us (10%)
  matrix products  25.6 us (7%)
  waiting for transfers between devices  19.5 us (5%)
  starting transfers between devices  16.5 us (5%)
  local copies, waits for them, and re-layouts  10.5 us (3%)
    reduce_sum x1, other arithmetic, on_device(): squares = jnp.sum(spectra * spectra, axis=(0, 2))  200 us
    convert_element_type x1, other arithmetic, polyphase(): samples = (voltages * input_mask[:, None, None]).astype(jnp.bfloat16)  40.1 us
    psum x1, blocking collectives, on_device(): band_total = lax.psum(band_partial, 'chan')  34.9 us
    ppermute x15, starting transfers between devices, rotated_exchange(): lax.ppermute(sent, axis, [(i, (i + step) % size) for i in range(size)])  14.9 us
    dot_general x1, matrix products, on_device(): jnp.einsum('isn,nk->iks', filtered, dft_matrix(NFFT, channels), preferred...  14.6 us
    ppermute x1, waiting for transfers between devices, swapped(): lax.ppermute(value, axis, [(i, i ^ 1 << stride) for i in range(lax.axis_s...  13.1 us
    dot_general x2, matrix products, contract(): lax.dot_general(left, right, (((1,), (1,)), ((), ())), preferred_element_...  10.9 us
    convert_element_type x1, other arithmetic, on_device(): return (summed / SPEC).astype(jnp.bfloat16)  9.98 us
  transfers between devices with their start and end apart: 16, of which 3 were waited for; matrix products, arithmetic and copies ran while one was open for 0% of the time, Pallas kernels for 0%

profile of v1, /device:TPU:0, one launch (start us, length us, event | category | flops | bytes accessed | tf_op | source)
XLA Modules:
  0.0 359.0 jit_solution(17937786244189427625)
XLA Ops:
  0.0 1.9 fusion.19
  1.9 1.0 cosine_convert_fusion
  2.8 40.1 %multiply_convert_fusion = bf16[128,79,2048]{2,0,1:T(8,128)(2,1)} fusion(s32[128,79,2048]{2,0,1:T(8,128)} %param.3, s32[128]{0:T(128)} %param.4), kind=kLoop, calls=%fused_computation.1 | loop fusion | flops 41418752 | bytes 124256768 | tf_op jit(solution)/shard_map/convert_element_type | solution.py:55
  43.0 200.3 %add_convert_fusion.1.clone.5 = bf16[128,64,2048]{2,0,1:T(8,128)(2,1)} fusion(bf16[128,79,2048]{2,0,1:T(8,128)(2,1)} %multiply_convert_fusion, f32[2048]{0:T(1024)S(1)} %bitcast.124, f32[2048]{0:T(1024)S(1)} %bitcast.125, f32[2048]{0:T(1024)S(1)} %bitcast.111, f32[2048]{0:T(1024)S(1)} %bitcast.112, f32[2048]{0:T(1024)S(1)} %bitcast.113, ...), kind=kLoop, calls=%fused_computation.2.clone.clone.clone.clone.2 | loop fusion | flops 805306368 | bytes 570556416 | tf_op jit(solution)/shard_map/reduce_sum | solution.py:78
  243.3 14.6 %multiply_reduce_fusion = (f32[16]{0:T(128)S(1)}, f32[16,128,64]{1,0,2:T(8,128)S(1)}) fusion(bf16[2048,8]{0,1:T(8,128)(2,1)S(1)} %copy-done.1, bf16[2048,8]{0,1:T(8,128)(2,1)S(1)} %copy-done, bf16[128,64,2048]{2,0,1:T(8,128)(2,1)} %add_convert_fusion.1.clone.5), kind=kOutput, calls=%fused_computation.8 | convolution fusion | flops 537264128 | bytes 34144320 | tf_op jit(solution)/shard_map/isn,nk->iks/dot_general | solution.py:75
  258.0 34.9 %psum.7 = f32[8]{0:T(128)S(1)} all-reduce(f32[8]{0:T(128)S(1)} %slice_add_fusion), channel_id=1, replica_groups=mesh['groups'=2,'chan'=16] {'chan'}, use_global_device_ids=true, to_apply=%region_1.2 | all-reduce | flops 8 | bytes 64 | tf_op jit(solution)/shard_map/psum | solution.py:80
  293.0 0.1 multiply_convert_fusion.2
  293.6 0.8 collective-permute-start.4
  294.5 4.8 %collective-permute-done = bf16[1,128,64]{1,2,0:T(8,128)(2,1)S(1)} collective-permute-done((bf16[1,128,64]{1,2,0:T(8,128)(2,1)S(1)}, bf16[1,128,64]{1,2,0:T(8,128)(2,1)S(1)}, u32[]{:S(2)}, u32[]{:S(2)}) %collective-permute-start) | collective-permute-done | bytes 16416 | tf_op jit(solution)/shard_map/ppermute | solution.py:33
  299.3 1.0 collective-permute-start.5
  300.3 3.2 collective-permute-start.7
  303.6 2.7 collective-permute-start.9
  306.3 3.2 collective-permute-start.10
  309.6 1.5 collective-permute-start.12
  311.1 1.4 collective-permute-start.13
  312.5 0.7 collective-permute-start.14
  313.4 1.5 collective-permute-done.13
  314.9 0.6 gather_fusion
  315.5 2.4 fusion.17
  317.9 8.6 %fusion.1 = f32[2048,2048]{1,0:T(8,128)} fusion(f32[2048,2048]{1,0:T(8,128)S(1)} %fusion.17, bf16[2048,32]{0,1:T(8,128)(2,1)S(1)} %get-tuple-element.6, bf16[2048,32]{0,1:T(8,128)(2,1)S(1)} %get-tuple-element.5, bf16[16,128,64]{1,2,0:T(8,128)(2,1)S(1)} %gather_fusion), kind=kOutput, calls=%fused_computation.5 | convolution fusion | flops 545783808 | bytes 34078720 | tf_op jit(solution)/shard_map/dot_general | solution.py:65
  326.5 7.7 %constant_dynamic-slice_fusion = f32[1024,2048]{1,0:T(8,128)} fusion(f32[2048,2048]{1,0:T(8,128)} %fusion.1, s32[]{:T(128)S(6)} %select_n.193), kind=kLoop, calls=%fused_computation.59 | loop fusion | bytes 16777220 | tf_op jit(solution)/shard_map/dynamic_slice | solution.py:100
  334.2 1.7 collective-permute-start.15
  335.9 13.1 %collective-permute-done.15 = f32[1024,2048]{1,0:T(8,128)} collective-permute-done((f32[1024,2048]{1,0:T(8,128)}, f32[1024,2048]{1,0:T(8,128)}, u32[]{:S(2)}, u32[]{:S(2)}) %collective-permute-start.15) | collective-permute-done | bytes 8388640 | tf_op jit(solution)/shard_map/ppermute | solution.py:39
  349.0 10.0 %multiply_convert_fusion.1 = bf16[1024,2048]{1,0:T(8,128)(2,1)} fusion(f32[1024,2048]{1,0:T(8,128)} %collective-permute-done.15, f32[2048,2048]{1,0:T(8,128)} %fusion.1, s32[]{:T(128)S(6)} %select_n.192), kind=kLoop, calls=%fused_computation.6 | loop fusion | flops 6291456 | bytes 20971524 | tf_op jit(solution)/shard_map/convert_element_type | solution.py:103
  (49 shorter events, 0.8 us)
Async XLA Ops:
  42.9 200.3 %copy-start = (bf16[2048,8]{0,1:T(8,128)(2,1)S(1)}, bf16[2048,8]{0,1:T(8,128)(2,1)}, u32[]{:S(2)}) copy-start(bf16[2048,8]{0,1:T(8,128)(2,1)} %get-tuple-element.39) | copy-start | bytes 98308
  43.0 200.3 %copy-start.1 = (bf16[2048,8]{0,1:T(8,128)(2,1)S(1)}, bf16[2048,8]{0,1:T(8,128)(2,1)}, u32[]{:S(2)}) copy-start(bf16[2048,8]{0,1:T(8,128)(2,1)} %get-tuple-element.40) | copy-start | bytes 98308
  293.4 5.9 %collective-permute-start = (bf16[1,128,64]{1,2,0:T(8,128)(2,1)S(1)}, bf16[1,128,64]{1,2,0:T(8,128)(2,1)S(1)}, u32[]{:S(2)}, u32[]{:S(2)}) collective-permute-start(bf16[1,128,64]{1,2,0:T(8,128)(2,1)S(1)} %get-tuple-element.21), channel_id=1, source_target_pairs={{0,1},{1,2},{2,3},{3,4},{4,5},{5,6},{6,7},{7,8},{8,9},{9,10},{10,1... | collective-permute-start | bytes 49160 | tf_op jit(solution)/shard_map/ppermute | solution.py:33
  293.4 6.9 %collective-permute-start.1 = (bf16[1,128,64]{1,2,0:T(8,128)(2,1)S(1)}, bf16[1,128,64]{1,2,0:T(8,128)(2,1)S(1)}, u32[]{:S(2)}, u32[]{:S(2)}) collective-permute-start(bf16[1,128,64]{1,2,0:T(8,128)(2,1)S(1)} %get-tuple-element.20), channel_id=1, source_target_pairs={{0,2},{1,3},{2,4},{3,5},{4,6},{5,7},{6,8},{7,9},{8,10},{9,11},{10,... | collective-permute-start | bytes 49160 | tf_op jit(solution)/shard_map/ppermute | solution.py:33
  293.5 6.8 %collective-permute-start.2 = (bf16[1,128,64]{1,2,0:T(8,128)(2,1)S(1)}, bf16[1,128,64]{1,2,0:T(8,128)(2,1)S(1)}, u32[]{:S(2)}, u32[]{:S(2)}) collective-permute-start(bf16[1,128,64]{1,2,0:T(8,128)(2,1)S(1)} %get-tuple-element.19), channel_id=1, source_target_pairs={{0,3},{1,4},{2,5},{3,6},{4,7},{5,8},{6,9},{7,10},{8,11},{9,12},{10... | collective-permute-start | bytes 49160 | tf_op jit(solution)/shard_map/ppermute | solution.py:33
  293.6 10.0 %collective-permute-start.3 = (bf16[1,128,64]{1,2,0:T(8,128)(2,1)S(1)}, bf16[1,128,64]{1,2,0:T(8,128)(2,1)S(1)}, u32[]{:S(2)}, u32[]{:S(2)}) collective-permute-start(bf16[1,128,64]{1,2,0:T(8,128)(2,1)S(1)} %get-tuple-element.18), channel_id=1, source_target_pairs={{0,4},{1,5},{2,6},{3,7},{4,8},{5,9},{6,10},{7,11},{8,12},{9,13},{1... | collective-permute-start | bytes 49160 | tf_op jit(solution)/shard_map/ppermute | solution.py:33
  293.6 10.0 %collective-permute-start.4 = (bf16[1,128,64]{1,2,0:T(8,128)(2,1)S(1)}, bf16[1,128,64]{1,2,0:T(8,128)(2,1)S(1)}, u32[]{:S(2)}, u32[]{:S(2)}) collective-permute-start(bf16[1,128,64]{1,2,0:T(8,128)(2,1)S(1)} %get-tuple-element.17), channel_id=1, source_target_pairs={{0,5},{1,6},{2,7},{3,8},{4,9},{5,10},{6,11},{7,12},{8,13},{9,14},{... | collective-permute-start | bytes 49160 | tf_op jit(solution)/shard_map/ppermute | solution.py:33
  299.3 7.0 %collective-permute-start.5 = (bf16[1,128,64]{1,2,0:T(8,128)(2,1)S(1)}, bf16[1,128,64]{1,2,0:T(8,128)(2,1)S(1)}, u32[]{:S(2)}, u32[]{:S(2)}) collective-permute-start(bf16[1,128,64]{1,2,0:T(8,128)(2,1)S(1)} %get-tuple-element.16), channel_id=1, source_target_pairs={{0,6},{1,7},{2,8},{3,9},{4,10},{5,11},{6,12},{7,13},{8,14},{9,15},... | collective-permute-start | bytes 49160 | tf_op jit(solution)/shard_map/ppermute | solution.py:33
  300.3 9.3 %collective-permute-start.6 = (bf16[1,128,64]{1,2,0:T(8,128)(2,1)S(1)}, bf16[1,128,64]{1,2,0:T(8,128)(2,1)S(1)}, u32[]{:S(2)}, u32[]{:S(2)}) collective-permute-start(bf16[1,128,64]{1,2,0:T(8,128)(2,1)S(1)} %get-tuple-element.15), channel_id=1, source_target_pairs={{0,7},{1,8},{2,9},{3,10},{4,11},{5,12},{6,13},{7,14},{8,15},{9,0},... | collective-permute-start | bytes 49160 | tf_op jit(solution)/shard_map/ppermute | solution.py:33
  300.3 9.3 %collective-permute-start.7 = (bf16[1,128,64]{1,2,0:T(8,128)(2,1)S(1)}, bf16[1,128,64]{1,2,0:T(8,128)(2,1)S(1)}, u32[]{:S(2)}, u32[]{:S(2)}) collective-permute-start(bf16[1,128,64]{1,2,0:T(8,128)(2,1)S(1)} %get-tuple-element.14), channel_id=1, source_target_pairs={{0,8},{1,9},{2,10},{3,11},{4,12},{5,13},{6,14},{7,15},{8,0},{9,1},... | collective-permute-start | bytes 49160 | tf_op jit(solution)/shard_map/ppermute | solution.py:33
  303.6 7.5 %collective-permute-start.8 = (bf16[1,128,64]{1,2,0:T(8,128)(2,1)S(1)}, bf16[1,128,64]{1,2,0:T(8,128)(2,1)S(1)}, u32[]{:S(2)}, u32[]{:S(2)}) collective-permute-start(bf16[1,128,64]{1,2,0:T(8,128)(2,1)S(1)} %get-tuple-element.13), channel_id=1, source_target_pairs={{0,9},{1,10},{2,11},{3,12},{4,13},{5,14},{6,15},{7,0},{8,1},{9,2},... | collective-permute-start | bytes 49160 | tf_op jit(solution)/shard_map/ppermute | solution.py:33
  303.6 8.9 %collective-permute-start.9 = (bf16[1,128,64]{1,2,0:T(8,128)(2,1)S(1)}, bf16[1,128,64]{1,2,0:T(8,128)(2,1)S(1)}, u32[]{:S(2)}, u32[]{:S(2)}) collective-permute-start(bf16[1,128,64]{1,2,0:T(8,128)(2,1)S(1)} %get-tuple-element.12), channel_id=1, source_target_pairs={{0,10},{1,11},{2,12},{3,13},{4,14},{5,15},{6,0},{7,1},{8,2},{9,3},... | collective-permute-start | bytes 49160 | tf_op jit(solution)/shard_map/ppermute | solution.py:33
  306.3 7.0 %collective-permute-start.10 = (bf16[1,128,64]{1,2,0:T(8,128)(2,1)S(1)}, bf16[1,128,64]{1,2,0:T(8,128)(2,1)S(1)}, u32[]{:S(2)}, u32[]{:S(2)}) collective-permute-start(bf16[1,128,64]{1,2,0:T(8,128)(2,1)S(1)} %get-tuple-element.11), channel_id=1, source_target_pairs={{0,11},{1,12},{2,13},{3,14},{4,15},{5,0},{6,1},{7,2},{8,3},{9,4},{... | collective-permute-start | bytes 49160 | tf_op jit(solution)/shard_map/ppermute | solution.py:33
  309.6 3.7 %collective-permute-start.11 = (bf16[1,128,64]{1,2,0:T(8,128)(2,1)S(1)}, bf16[1,128,64]{1,2,0:T(8,128)(2,1)S(1)}, u32[]{:S(2)}, u32[]{:S(2)}) collective-permute-start(bf16[1,128,64]{1,2,0:T(8,128)(2,1)S(1)} %get-tuple-element.10), channel_id=1, source_target_pairs={{0,12},{1,13},{2,14},{3,15},{4,0},{5,1},{6,2},{7,3},{8,4},{9,5},{1... | collective-permute-start | bytes 49160 | tf_op jit(solution)/shard_map/ppermute | solution.py:33
  309.6 3.7 %collective-permute-start.12 = (bf16[1,128,64]{1,2,0:T(8,128)(2,1)S(1)}, bf16[1,128,64]{1,2,0:T(8,128)(2,1)S(1)}, u32[]{:S(2)}, u32[]{:S(2)}) collective-permute-start(bf16[1,128,64]{1,2,0:T(8,128)(2,1)S(1)} %get-tuple-element.9), channel_id=1, source_target_pairs={{0,13},{1,14},{2,15},{3,0},{4,1},{5,2},{6,3},{7,4},{8,5},{9,6},{10... | collective-permute-start | bytes 49160 | tf_op jit(solution)/shard_map/ppermute | solution.py:33
  311.1 3.7 %collective-permute-start.13 = (bf16[1,128,64]{1,2,0:T(8,128)(2,1)S(1)}, bf16[1,128,64]{1,2,0:T(8,128)(2,1)S(1)}, u32[]{:S(2)}, u32[]{:S(2)}) collective-permute-start(bf16[1,128,64]{1,2,0:T(8,128)(2,1)S(1)} %get-tuple-element.8), channel_id=1, source_target_pairs={{0,14},{1,15},{2,0},{3,1},{4,2},{5,3},{6,4},{7,5},{8,6},{9,7},{10,... | collective-permute-start | bytes 49160 | tf_op jit(solution)/shard_map/ppermute | solution.py:33
  312.5 2.3 collective-permute-start.14
  334.2 14.8 %collective-permute-start.15 = (f32[1024,2048]{1,0:T(8,128)}, f32[1024,2048]{1,0:T(8,128)}, u32[]{:S(2)}, u32[]{:S(2)}) collective-permute-start(f32[1024,2048]{1,0:T(8,128)} %constant_dynamic-slice_fusion), channel_id=1, source_target_pairs={{0,1},{1,0},{2,3},{3,2},{4,5},{5,4},{6,7},{7,6},{8,9},{9,8},{10,11... | collective-permute-start | bytes 25165832 | tf_op jit(solution)/shard_map/ppermute | solution.py:39
